TPU v7x, 512 devices: a whole 4x8x8 slice. The times are simulated.
512 devices in a mesh: inner: 16 (over z_hi, x, core), outer: 32 (over y, z_lo).
Axes of the slice: x: 4, y: 8, z: 8 (z_hi: 2, z_lo: 4; z = z_hi * 4 + z_lo), core: 2. Of those that a mesh axis runs over, the one named last changes fastest.
Arguments:
- acts: bfloat16 [65536, 8192], P(('inner', 'outer')), may hold values from -24 to 24
- cotangent: bfloat16 [65536, 8192], P(('inner', 'outer')), may hold values from -0.75 to 0.75
- latent_ids: int32 [65536, 4], P(('inner', 'outer')), may hold values from 0 to 255, all different within a row
- enc_rows: bfloat16 [256, 8192], P('inner'), may hold values from -0.0625 to 0.0625
- dec_rows: bfloat16 [256, 8192], P('inner'), may hold values from -0.0625 to 0.0625
Outputs:
- enc_grad: float32 [256, 8192], P('outer', 'inner')
- dec_grad: float32 [256, 8192], P('outer', 'inner')
Inputs may be any that keep to these rules, and one draw needn't show every extreme that they name: `latent_ids`: each row names 4 different latents; every latent is named by some row.
All inputs are finite; a program needn't handle non-finite values.
Results may differ from a plain program's by a relative error of at most 0.0095.
Values may be sent and summed in bfloat16 or wider, within the bound.
A program may use at most 64 MiB of HBM per device.

v0:
```python
import jax
import jax.numpy as jnp
from jax import lax
from jax.sharding import PartitionSpec as P


def against_rows(left, rows):
    return lax.dot_general(left, rows, (((1,), (1,)), ((), ())), preferred_element_type=jnp.float32)


def local(acts, cotangent, latent_ids, enc_rows, dec_rows):
    latents = enc_rows.shape[0] * lax.axis_size("inner")
    pre = against_rows(acts, lax.all_gather(enc_rows, "inner", axis=0, tiled=True))
    back = against_rows(cotangent, lax.all_gather(dec_rows, "inner", axis=0, tiled=True))
    columns = jnp.arange(latents, dtype=jnp.int32)
    mask = jnp.any(latent_ids[:, :, None] == columns[None, None, :], axis=1).astype(jnp.float32)
    codes = (pre * mask).astype(jnp.bfloat16)
    dcodes = (back * mask).astype(jnp.bfloat16)
    over_tokens = (((0,), (0,)), ((), ()))
    term_enc = lax.dot_general(dcodes, acts, over_tokens, preferred_element_type=jnp.float32)
    term_dec = lax.dot_general(codes, cotangent, over_tokens, preferred_element_type=jnp.float32)
    values = jnp.stack([term_enc, term_dec])[None].astype(jnp.bfloat16)
    received = lax.all_to_all(values, "inner", split_axis=3, concat_axis=0, tiled=True)
    section_sum = jnp.sum(received.astype(jnp.float32), axis=0)
    received = lax.all_to_all(
        section_sum[None].astype(jnp.bfloat16), "outer", split_axis=2, concat_axis=0, tiled=True
    )
    total = jnp.sum(received.astype(jnp.float32), axis=0)
    return (total[0], total[1])


def solution(mesh):
    placed = (
        P(("inner", "outer"), None),
        P(("inner", "outer"), None),
        P(("inner", "outer"), None),
        P("inner", None),
        P("inner", None),
    )
    return jax.shard_map(
        local,
        mesh=mesh,
        in_specs=placed,
        out_specs=(P("outer", "inner"), P("outer", "inner")),
        check_vma=False,
    )
```

profile of v0, /device:TPU:1, one launch (start us, length us, event | category | flops | bytes accessed | tf_op | source)
XLA Modules:
  0.0 455.0 jit_solution(11454028703203108922)
XLA Ops:
  7.2 0.0 copy-start
  7.2 0.0 all-gather.5.cloned.1.call-start
  7.2 0.7 all-gather.5.cloned.1.call-update
  7.9 0.0 all-gather.3.cloned.1.call-start
  8.0 0.7 all-gather.3.cloned.1.call-update
  8.7 0.8 fusion.4
  9.5 91.0 %all-gather.5.cloned.1.call-done = bf16[256,8192]{1,0:T(8,128)(2,1)} async-done(((bf16[16,8192]{1,0:T(8,128)(2,1)}), bf16[256,8192]{1,0:T(8,128)(2,1)}) %all-gather.5.cloned.1.call-update) | async-done | bytes 4194320 | tf_op jit(solution)/shard_map/all_gather | solution.py:13
  100.5 0.0 copy-done
  100.5 9.6 %fusion.1 = bf16[1,1,256,8192]{3,2,1,0:T(8,128)(2,1)} fusion(bf16[128,8192]{1,0:T(8,128)(2,1)S(1)} %copy-done, pred[128,256]{1,0:T(8,128)(4,1)S(1)} %fusion.4, bf16[128,8192]{1,0:T(8,128)(2,1)} %param.5, bf16[256,8192]{1,0:T(8,128)(2,1)} %all-gather.5.cloned.1.call-done), kind=kOutput, calls=%fused_computation.3 | convolution fusion | flops 1075904512 | bytes 12615680 | tf_op jit(solution)/shard_map/dot_general | solution.py:21
  110.0 72.7 %all-gather.3.cloned.1.call-done = bf16[256,8192]{1,0:T(8,128)(2,1)} async-done(((bf16[16,8192]{1,0:T(8,128)(2,1)}), bf16[256,8192]{1,0:T(8,128)(2,1)}) %all-gather.3.cloned.1.call-update) | async-done | bytes 4194320 | tf_op jit(solution)/shard_map/all_gather | solution.py:14
  182.7 9.6 %fusion = bf16[1,1,256,8192]{3,2,1,0:T(8,128)(2,1)} fusion(bf16[128,8192]{1,0:T(8,128)(2,1)} %param.5, pred[128,256]{1,0:T(8,128)(4,1)S(1)} %fusion.4, bf16[128,8192]{1,0:T(8,128)(2,1)S(1)} %copy-done, bf16[256,8192]{1,0:T(8,128)(2,1)} %all-gather.3.cloned.1.call-done), kind=kOutput, calls=%fused_computation.2 | convolution fusion | flops 1075904512 | bytes 12615680 | tf_op jit(solution)/shard_map/dot_general | solution.py:20
  192.3 7.4 %pad_maximum_fusion = bf16[1,2,256,8192]{3,2,1,0:T(8,128)(2,1)} fusion(bf16[1,1,256,8192]{3,2,1,0:T(8,128)(2,1)} %fusion.1, bf16[1,1,256,8192]{3,2,1,0:T(8,128)(2,1)} %fusion), kind=kLoop, calls=%fused_computation.4 | loop fusion | flops 4194304 | bytes 16777216 | tf_op jit(solution)/shard_map/stack | solution.py:22
  199.7 21.0 %copy.13 = bf16[1,2,256,8192]{2,1,0,3:T(2,128)(2,1)} copy(bf16[1,2,256,8192]{3,2,1,0:T(8,128)(2,1)} %pad_maximum_fusion) | data formatting | bytes 16777216 | tf_op jit(solution)/shard_map/stack | solution.py:22
  220.8 193.0 %all_to_all.21 = bf16[1,2,256,8192]{2,1,0,3:T(2,128)(2,1)} all-to-all(bf16[1,2,256,8192]{2,1,0,3:T(2,128)(2,1)} %copy.13), channel_id=1, replica_groups=mesh['inner'=16,'outer'=32] {'inner'}, dimensions={3} | all-to-all | bytes 16777216 | tf_op jit(solution)/shard_map/all_to_all | solution.py:23
  413.8 8.7 %reduce_sum.21 = bf16[2,256,512]{1,0,2:T(2,128)(2,1)S(1)} reduce(bf16[2,256,16,512]{1,0,3,2:T(2,128)(2,1)} %bitcast.18, bf16[]{:T(256)} %constant.7.clone.1), dimensions={2}, to_apply=%region_1.0 | reduce | flops 3932160 | bytes 8912898 | tf_op jit(solution)/shard_map/reduce_sum | solution.py:24
  422.5 1.1 copy.14
  423.6 23.5 %all_to_all.22 = bf16[1,2,256,512]{3,1,0,2:T(2,128)(2,1)S(1)} all-to-all(bf16[1,2,256,512]{3,1,0,2:T(2,128)(2,1)S(1)} %copy.14), channel_id=1, replica_groups=mesh['inner'=16,'outer'=32] {'outer'}, dimensions={2} | all-to-all | bytes 1048576 | tf_op jit(solution)/shard_map/all_to_all | solution.py:25
  447.1 0.4 convert_reduce_fusion
  447.6 0.6 copy_bitcast_fusion
  (1 shorter events, 0.0 us)
Async XLA Ops:
  7.2 93.3 %copy-start = (bf16[128,8192]{1,0:T(8,128)(2,1)S(1)}, bf16[128,8192]{1,0:T(8,128)(2,1)}, u32[]{:S(2)}) copy-start(bf16[128,8192]{1,0:T(8,128)(2,1)} %param.6) | copy-start | bytes 6291460
  7.2 93.3 %all-gather.5.cloned.1.call-start = ((), (), s32[]{:S(2)}) async-start(), calls=%async_computation.3 | async-start | bytes 4456448 | tf_op jit(solution)/shard_map/all_gather | solution.py:13
  7.9 174.8 %all-gather.3.cloned.1.call-start = ((), (), s32[]{:S(2)}) async-start(), calls=%async_computation.2 | async-start | bytes 4456448 | tf_op jit(solution)/shard_map/all_gather | solution.py:14
Sparse Core Ops, SparseCore 0:
  11.3 89.0 all-gather.4
  103.8 78.8 all-gather.2
where the time goes:
time: 457 us; the launch traced here: 455 us
  blocking collectives  217 us (47%)
  waiting for transfers between devices  165 us (36%)
  local copies, waits for them, and re-layouts  22.8 us (5%)
  matrix products  19.1 us (4%)
  other arithmetic  17.4 us (4%)
  between operations  14.1 us (3%)
    all_to_all x1, blocking collectives, local(): lax.all_to_all(values, 'inner', split_axis=3, concat_axis=0, tiled=True)  193 us
    all_gather x1, waiting for transfers between devices, local(): lax.all_gather(enc_rows, 'inner', axis=0, tiled=True)  91 us
    all_gather x1, waiting for transfers between devices, local(): lax.all_gather(dec_rows, 'inner', axis=0, tiled=True)  72.7 us
    all_to_all x1, blocking collectives, local(): lax.all_to_all(section_sum[None].astype(jnp.bfloat16), 'outer', split_axi...  23.5 us
    another operation x1, local copies, waits for them, and re-layouts, local(): values = jnp.stack([term_enc, term_dec])[None].astype(jnp.bfloat16)  21 us
    dot_general x1, matrix products, local(): lax.dot_general(dcodes, acts, over_tokens, preferred_element_type=jnp.flo...  9.58 us
    dot_general x1, matrix products, local(): lax.dot_general(codes, cotangent, over_tokens, preferred_element_type=jnp...  9.56 us
  transfers between devices with their start and end apart: 2, of which 2 were waited for; matrix products, arithmetic and copies ran while one was open for 2% of the time, Pallas kernels for 0%

commit v1 on v0

v1 whole, which is shorter than its diff:
```python
import functools

import jax
import jax.numpy as jnp
from jax import lax
from jax.experimental import pallas as pl
from jax.experimental.pallas import tpu as pltpu
from jax.sharding import PartitionSpec as P

MESH = pl.DeviceIdType.MESH
PIECES = 2
NX, NY, NZ, NZL = 4, 8, 8, 4
GROUP = 16
CUBES = 32
TOK, LB, BLOCK = 128, 256, 512
K = 4


def div(a, b):
    return lax.div(jnp.int32(a), jnp.int32(b))


def rem(a, b):
    return lax.rem(jnp.int32(a), jnp.int32(b))


def place():
    inner, outer = lax.axis_index("inner"), lax.axis_index("outer")
    zh, x, c = div(inner, 8), rem(div(inner, 2), 4), rem(inner, 2)
    y, zl = div(outer, 4), rem(outer, 4)
    return x, y, zh * 4 + zl, c


def device(x, y, z, c):
    return (div(z, 4) * 8 + x * 2 + c, y * 4 + rem(z, 4))


def block_of(x, y, z, c):
    return rem(z, 2) * 8 + rem(y, 2) * 4 + rem(x, 2) * 2 + c


def step(v, s):
    return (1 - 2 * rem(v, 2)) * (1 - 2 * s)


def peer(s, d):
    x, y, z, c = place()
    dx, dy, dz, dc = div(d, 8), rem(div(d, 4), 2), rem(div(d, 2), 2), rem(d, 2)
    return (
        rem(x + dx * step(x, s) + NX, NX),
        rem(y + dy * step(y, s) + NY, NY),
        rem(z + dz * step(z, s) + NZ, NZ),
        rem(c + dc, 2),
    )


def kernel(acts, cot, ids, enc, dec, oenc, odec,
           tok, rows, idsb, pout, pin, cout, cin, spread, tsend, fin,
           tok_s, tok_r, row_s, row_r, ids_s, ids_r, p_s, p_r, c_s, c_r, f_s, f_r):
    W = BLOCK // PIECES
    x, y, z, c = place()
    inner = lax.axis_index("inner")
    me = device(x, y, z, c)
    mine = block_of(x, y, z, c)
    zl = rem(z, 4)

    def inner_peer(e):
        i = rem(inner + e, 16)
        return i, (i, y * 4 + zl)

    def source(k):
        x1 = 2 * div(k, 16) + rem(x, 2)
        y1 = 2 * rem(div(k, 4), 4) + div(x, 2)
        z1 = 2 * rem(k, 4) + div(z, 4)
        return device(x1, y1, z1, c)

    barrier = pltpu.get_barrier_semaphore()

    @pl.loop(1, GROUP)
    def _(d):
        for s in range(PIECES):
            pl.semaphore_signal(barrier, inc=1, device_id=device(*peer(s, d)), device_id_type=MESH)
        pl.semaphore_signal(barrier, inc=1, device_id=inner_peer(d)[1], device_id_type=MESH)

    @pl.loop(0, CUBES)
    def _(k):
        src = source(k)

        @pl.when((src[0] != me[0]) | (src[1] != me[1]))
        def _():
            pl.semaphore_signal(barrier, inc=1, device_id=src, device_id_type=MESH)

    stays = (rem(z, 2) == div(z, 4)) & (rem(y, 2) * 2 + rem(x, 2) == x)
    pl.semaphore_wait(barrier, (GROUP - 1) * (PIECES + 1) + CUBES - stays.astype(jnp.int32))

    def columns(block, s):
        return pl.ds(pl.multiple_of(block * BLOCK + s * W, W), W)

    def ids_copy(s, d):
        return pltpu.make_async_remote_copy(
            src_ref=ids, dst_ref=idsb.at[s, d], send_sem=ids_s.at[s, d], recv_sem=ids_r.at[s, d],
            device_id=device(*peer(s, d)), device_id_type=MESH)

    def tok_copy(a, s, d):
        p = peer(s, d)
        return pltpu.make_async_remote_copy(
            src_ref=(acts, cot)[a].at[:, columns(block_of(*p), s)], dst_ref=tok.at[a, s, d],
            send_sem=tok_s.at[a, s, d], recv_sem=tok_r.at[a, s, d],
            device_id=device(*p), device_id_type=MESH)

    def own_tok(a, s):
        return pltpu.make_async_copy(
            (acts, cot)[a].at[:, columns(mine, s)], tok.at[a, s, 0], tok_r.at[a, s, 0])

    def row_copy(a, e):
        i, dev = inner_peer(e)
        block = rem(z, 2) * 8 + rem(y, 2) * 4 + rem(div(i, 2), 2) * 2 + rem(i, 2)
        return pltpu.make_async_remote_copy(
            src_ref=(enc, dec)[a].at[:, pl.ds(pl.multiple_of(block * BLOCK, BLOCK), BLOCK)],
            dst_ref=rows.at[a, pl.ds(pl.multiple_of(inner * 16, 16), 16), :],
            send_sem=row_s.at[a, e], recv_sem=row_r.at[a, e], device_id=dev, device_id_type=MESH)

    def own_row(a):
        return pltpu.make_async_copy(
            (enc, dec)[a].at[:, pl.ds(pl.multiple_of(mine * BLOCK, BLOCK), BLOCK)],
            rows.at[a, pl.ds(pl.multiple_of(inner * 16, 16), 16), :], row_r.at[a, 0])

    def part_copy(s, d):
        return pltpu.make_async_remote_copy(
            src_ref=pout.at[s, d], dst_ref=pin.at[s, d], send_sem=p_s.at[s, d], recv_sem=p_r.at[s, d],
            device_id=device(*peer(s, d)), device_id_type=MESH)

    def code_copy(s, d):
        return pltpu.make_async_remote_copy(
            src_ref=cout, dst_ref=cin.at[s, d], send_sem=c_s.at[s, d], recv_sem=c_r.at[s, d],
            device_id=device(*peer(s, d)), device_id_type=MESH)

    cube = div(x, 2) * 16 + div(y, 2) * 4 + div(z, 2)

    def final_dest(j):
        return (rem(z, 2) * 8 + (rem(y, 2) * 2 + rem(x, 2)) * 2 + c,
                rem(y + div(j, 4), 8) * 4 + rem(zl + rem(j, 4), 4))

    def final_copy(j):
        dev = final_dest(j)
        return pltpu.make_async_remote_copy(
            src_ref=tsend.at[dev[1]], dst_ref=fin.at[cube], send_sem=f_s.at[j], recv_sem=f_r.at[cube],
            device_id=dev, device_id_type=MESH)

    def own_final():
        return pltpu.make_async_copy(tsend.at[me[1]], fin.at[cube], f_s.at[0])

    for a in range(2):
        own_row(a).start()

    @pl.loop(1, 16)
    def _(e):
        for a in range(2):
            row_copy(a, e).start()
        for s in range(PIECES):
            ids_copy(s, e).start()

    for a in range(2):
        for s in range(PIECES):
            own_tok(a, s).start()

    @pl.loop(1, GROUP)
    def _(d):
        for s in range(PIECES):
            for a in range(2):
                tok_copy(a, s, d).start()

    for s in range(PIECES):
        idsb[s, 0] = ids[...]

    for a in range(2):
        own_row(a).wait()

    @pl.loop(1, 16)
    def _(e):
        for a in range(2):
            row_copy(a, e).wait_recv()

    latent = lax.broadcasted_iota(jnp.int32, (LB, TOK), 0)

    def partial(s, d):
        which = idsb[s, d]
        out = []
        for a in range(2):
            full = lax.dot_general(rows[a, :, s * W:(s + 1) * W], tok[a, s, d],
                                   (((1,), (1,)), ((), ())), preferred_element_type=jnp.float32)
            for k in range(K):
                out.append(jnp.sum(jnp.where(which[k:k + 1, :] == latent, full, 0.0), axis=0, keepdims=True))
        return jnp.concatenate(out, axis=0)

    for s in range(PIECES):
        for a in range(2):
            own_tok(a, s).wait()
        pin[s, 0] = partial(s, 0)

    @pl.loop(1, GROUP)
    def _(d):
        for s in range(PIECES):
            ids_copy(s, d).wait_recv()
            for a in range(2):
                tok_copy(a, s, d).wait_recv()
            pout[s, d] = partial(s, d)
            part_copy(s, d).start()

    @pl.loop(1, GROUP)
    def _(d):
        for s in range(PIECES):
            part_copy(s, d).wait_recv()

    codes = jnp.zeros((2 * K, TOK), jnp.float32)
    for s in range(PIECES):
        for d in range(GROUP):
            codes = codes + pin[s, d]
    cout[...] = codes.astype(jnp.bfloat16).astype(jnp.float32)

    @pl.loop(1, GROUP)
    def _(d):
        for s in range(PIECES):
            code_copy(s, d).start()

    for s in range(PIECES):
        cin[s, 0] = cout[...]

    def expand(s, d):
        which, values = idsb[s, d], cin[s, d]
        at = pl.ds(pl.multiple_of(d * TOK, TOK), TOK)
        for a in range(2):
            full = jnp.zeros((LB, TOK), jnp.float32)
            for k in range(K):
                full = jnp.where(which[k:k + 1, :] == latent, values[a * K + k:a * K + k + 1, :], full)
            spread[a, s, :, at] = full.astype(jnp.bfloat16)

    for s in range(PIECES):
        expand(s, 0)

    @pl.loop(1, GROUP)
    def _(d):
        for s in range(PIECES):
            code_copy(s, d).wait_recv()
            expand(s, d)

    for s in range(PIECES):
        terms = []
        for a in range(2):
            right = tok[a, s].reshape(GROUP * TOK, W)
            terms.append(lax.dot_general(spread[1 - a, s], right, (((1,), (0,)), ((), ())),
                                         preferred_element_type=jnp.float32).reshape(CUBES, 8, W))
        tsend[:, :, s * W:(s + 1) * W] = jnp.concatenate(terms, axis=1).astype(jnp.bfloat16)

    @pl.when(stays)
    def _():
        own_final().start()

    @pl.when(jnp.logical_not(stays))
    def _():
        final_copy(0).start()

    @pl.loop(1, CUBES)
    def _(j):
        final_copy(j).start()

    @pl.loop(1, GROUP)
    def _(d):
        for a in range(2):
            row_copy(a, d).wait_send()
        for s in range(PIECES):
            ids_copy(s, d).wait_send()
            part_copy(s, d).wait_send()
            code_copy(s, d).wait_send()
            for a in range(2):
                tok_copy(a, s, d).wait_send()

    @pl.when(stays)
    def _():
        own_final().wait()

    @pl.when(jnp.logical_not(stays))
    def _():
        final_copy(0).wait_send()

    @pl.loop(1, CUBES)
    def _(j):
        final_copy(j).wait_send()

    @pl.loop(0, CUBES)
    def _(k):
        @pl.when(jnp.logical_not(stays & (k == cube)))
        def _():
            pltpu.make_async_remote_copy(
                src_ref=tsend.at[0], dst_ref=fin.at[k], send_sem=f_s.at[0], recv_sem=f_r.at[k],
                device_id=me, device_id_type=MESH).wait_recv()

    total = jnp.zeros((16, BLOCK), jnp.float32)
    for k in range(CUBES):
        total = total + fin[k].astype(jnp.float32)
    oenc[...] = total[:8]
    odec[...] = total[8:]


def local(acts, cotangent, latent_ids, enc_rows, dec_rows):
    S, W = PIECES, BLOCK // PIECES
    ids = latent_ids.T
    ids = jnp.concatenate([ids, ids], axis=0)
    vmem, hbm = pl.BlockSpec(memory_space=pltpu.VMEM), pl.BlockSpec(memory_space=pl.ANY)
    dma = pltpu.SemaphoreType.DMA
    return pl.pallas_call(
        kernel,
        out_shape=(jax.ShapeDtypeStruct((8, BLOCK), jnp.float32),) * 2,
        in_specs=[hbm, hbm, vmem, hbm, hbm],
        out_specs=(vmem, vmem),
        scratch_shapes=[
            pltpu.VMEM((2, S, GROUP, TOK, W), jnp.bfloat16),
            pltpu.VMEM((2, LB, BLOCK), jnp.bfloat16),
            pltpu.VMEM((S, GROUP, 8, TOK), jnp.int32),
            pltpu.VMEM((S, GROUP, 8, TOK), jnp.float32),
            pltpu.VMEM((S, GROUP, 8, TOK), jnp.float32),
            pltpu.VMEM((8, TOK), jnp.float32),
            pltpu.VMEM((S, GROUP, 8, TOK), jnp.float32),
            pltpu.VMEM((2, S, LB, GROUP * TOK), jnp.bfloat16),
            pltpu.VMEM((CUBES, 16, BLOCK), jnp.bfloat16),
            pltpu.VMEM((CUBES, 16, BLOCK), jnp.bfloat16),
            dma((2, S, GROUP)), dma((2, S, GROUP)),
            dma((2, 16)), dma((2, 16)),
            dma((S, GROUP)), dma((S, GROUP)),
            dma((S, GROUP)), dma((S, GROUP)),
            dma((S, GROUP)), dma((S, GROUP)),
            dma((CUBES,)), dma((CUBES,)),
        ],
        compiler_params=pltpu.CompilerParams(
            collective_id=0, has_side_effects=True, vmem_limit_bytes=40 * 2**20),
    )(acts, cotangent, ids, enc_rows, dec_rows)


def solution(mesh):
    placed = (
        P(("inner", "outer"), None),
        P(("inner", "outer"), None),
        P(("inner", "outer"), None),
        P("inner", None),
        P("inner", None),
    )
    return jax.shard_map(
        local,
        mesh=mesh,
        in_specs=placed,
        out_specs=(P("outer", "inner"), P("outer", "inner")),
        check_vma=False,
    )
```

time: 457 us -> 101 us (0.22)
  blocking collectives: 217 us -> 0 us
  waiting for transfers between devices: 165 us -> 0 us
  Pallas kernels: 0 us -> 92.4 us
  matrix products: 19.1 us -> 0 us
  other arithmetic: 17.4 us -> 0.77 us
  local copies, waits for them, and re-layouts: 22.8 us -> 6.29 us
  between operations: 14.1 us -> 0.64 us
    all_to_all x2 -> x0, blocking collectives: 217 us -> none  [the longest x1 193 us: local(): lax.all_to_all(values, 'inner', split_axis=3, concat_axis=0, tiled=True)]
    all_gather x2 -> x0, waiting for transfers between devices: 164 us -> none  [the longest x1 91 us: local(): lax.all_gather(enc_rows, 'inner', axis=0, tiled=True)]
    pallas_call x0 -> x1, Pallas kernels: none -> 92.4 us  [local(): pl.pallas_call(kernel, out_shape=(jax.ShapeDtypeStruct((8, BLOCK), jnp.fl...]
    another operation x1 -> x0, local copies, waits for them, and re-layouts: 21 us -> none  [local(): values = jnp.stack([term_enc, term_dec])[None].astype(jnp.bfloat16)]
    dot_general x2 -> x0, matrix products: 19.1 us -> none  [the longest x1 9.58 us: local(): lax.dot_general(dcodes, acts, over_tokens, preferred_element_type=jnp.flo...]
    reduce_sum x2 -> x0, other arithmetic: 9.13 us -> none  [the longest x1 8.69 us: local(): section_sum = jnp.sum(received.astype(jnp.float32), axis=0)]
    another operation x1 -> x0, other arithmetic: 7.45 us -> none  [local(): values = jnp.stack([term_enc, term_dec])[None].astype(jnp.bfloat16)]
    unnamed x3 -> x10, local copies, waits for them, and re-layouts: 0.62 us -> 6.29 us
  transfers between devices with their start and end apart: 2 -> 0, of which waited for: 2 -> 0; matrix products, arithmetic and copies ran while one was open for 2% -> 0% of each run, Pallas kernels for 0% -> 0%
where the time goes in v1:
time: 101 us; the launch traced here: 100 us
  Pallas kernels  92.4 us (91%)
  local copies, waits for them, and re-layouts  6.29 us (6%)
    pallas_call x1, Pallas kernels, local(): pl.pallas_call(kernel, out_shape=(jax.ShapeDtypeStruct((8, BLOCK), jnp.fl...  92.4 us
    unnamed x10, local copies, waits for them, and re-layouts  6.29 us

profile of v1, /device:TPU:1, one launch (start us, length us, event | category | flops | bytes accessed | tf_op | source)
XLA Modules:
  0.0 100.1 jit_solution(11641629557808050869)
XLA Ops:
  0.6 0.8 pad_add_fusion.ids
  1.4 0.0 copy-start
  1.4 1.6 %copy-done = bf16[128,8192]{1,0:T(8,128)(2,1)S(1)} copy-done((bf16[128,8192]{1,0:T(8,128)(2,1)S(1)}, bf16[128,8192]{1,0:T(8,128)(2,1)}, u32[]{:S(2)}) %copy-start) | copy-done | bytes 2097176
  3.0 0.0 copy-start.1
  3.0 1.6 %copy-done.1 = bf16[128,8192]{1,0:T(8,128)(2,1)S(1)} copy-done((bf16[128,8192]{1,0:T(8,128)(2,1)S(1)}, bf16[128,8192]{1,0:T(8,128)(2,1)}, u32[]{:S(2)}) %copy-start.1) | copy-done | bytes 2097176
  4.6 0.0 copy-start.2
  4.6 0.9 copy-done.2
  5.5 0.0 copy-start.3
  5.5 0.9 copy-done.3
  6.5 92.4 %shard_map.68 = (f32[8,512]{1,0:T(8,128)S(1)}, f32[8,512]{1,0:T(8,128)S(1)}) custom-call(bf16[128,8192]{1,0:T(8,128)(2,1)S(1)} %copy-done, bf16[128,8192]{1,0:T(8,128)(2,1)S(1)} %copy-done.1, s32[8,128]{1,0:T(8,128)S(1)} %pad_add_fusion.ids, bf16[16,8192]{1,0:T(8,128)(2,1)S(1)} %copy-done.2, bf16[16,8192]{1,0:T(8,128)(2,1)S(1)} %copy-done.3), custom_call_target="tpu_custom_call" | custom-call | tf_op jit(solution)/shard_map/pallas_call | solution.py:311
  98.9 0.6 copy.9
  99.5 0.6 copy.10
Async XLA Ops:
  1.4 1.6 %copy-start = (bf16[128,8192]{1,0:T(8,128)(2,1)S(1)}, bf16[128,8192]{1,0:T(8,128)(2,1)}, u32[]{:S(2)}) copy-start(bf16[128,8192]{1,0:T(8,128)(2,1)} %acts.1) | copy-start | bytes 6291460
  3.0 1.6 %copy-start.1 = (bf16[128,8192]{1,0:T(8,128)(2,1)S(1)}, bf16[128,8192]{1,0:T(8,128)(2,1)}, u32[]{:S(2)}) copy-start(bf16[128,8192]{1,0:T(8,128)(2,1)} %cot.1) | copy-start | bytes 6291460
  4.6 0.9 copy-start.2
  5.5 0.9 copy-start.3

commit v2 on v0

v2 whole, which is shorter than its diff:
```python
import functools

import jax
import jax.numpy as jnp
from jax import lax
from jax.experimental import pallas as pl
from jax.experimental.pallas import tpu as pltpu
from jax.sharding import PartitionSpec as P

MESH = pl.DeviceIdType.MESH
PIECES = 2
NX, NY, NZ = 4, 8, 8
GROUP = 16
CUBES = 32
TOK, LB, BLOCK = 128, 256, 512
K = 4
PEERS = sorted(range(1, GROUP), key=lambda d: (-bin(d >> 1).count("1"), d))


def div(a, b):
    return lax.div(a, jnp.int32(b))


def rem(a, b):
    return lax.rem(a, jnp.int32(b))


def towards(v, s, n):
    return rem(v + (1 - 2 * rem(v, 2)) * (1 - 2 * s) + n, n)


def kernel(acts, cot, ids, enc, dec, oenc, odec,
           tok, rows, idsb, pout, pin, cout, cin, spread, tsend, fin,
           tok_s, tok_r, row_s, row_r, ids_s, ids_r, p_s, p_r, c_s, c_r, f_s, f_r):
    W = BLOCK // PIECES
    inner, outer = lax.axis_index("inner"), lax.axis_index("outer")
    zh, x, c = div(inner, 8), rem(div(inner, 2), 4), rem(inner, 2)
    y, zl = div(outer, 4), rem(outer, 4)
    z = zh * 4 + zl
    me = (inner, outer)
    px, py, pz = rem(x, 2), rem(y, 2), rem(z, 2)
    pieces = range(PIECES)

    cs = (c, 1 - c)
    x2 = [(x * 2, towards(x, s, NX) * 2) for s in pieces]
    y4 = [(y * 4, towards(y, s, NY) * 4) for s in pieces]
    zz = [(z, towards(z, s, NZ)) for s in pieces]
    z8 = [tuple(div(v, 4) * 8 for v in pair) for pair in zz]
    zr = [tuple(rem(v, 4) for v in pair) for pair in zz]
    xc = [[[x2[s][dx] + cs[dc] for dc in range(2)] for dx in range(2)] for s in pieces]
    bx, by, bz = (px * 2, 2 - px * 2), (py * 4, 4 - py * 4), (pz * 8, 8 - pz * 8)
    bxc = [[bx[dx] + cs[dc] for dc in range(2)] for dx in range(2)]
    byz = [[by[dy] + bz[dz] for dz in range(2)] for dy in range(2)]

    def bits(d):
        return d >> 3, (d >> 2) & 1, (d >> 1) & 1, d & 1

    def peer(s, d):
        dx, dy, dz, dc = bits(d)
        return z8[s][dz] + xc[s][dx][dc], y4[s][dy] + zr[s][dz]

    def block(d):
        dx, dy, dz, dc = bits(d)
        return bxc[dx][dc] + byz[dy][dz]

    inner_at = [inner] + [rem(inner + e, 16) for e in range(1, 16)]

    def inner_block(e):
        return rem(inner_at[e], 4) + byz[0][0]

    mx, my = px, div(x, 2)
    src_x = [(2 * kx + mx) * 2 + c for kx in range(2)]
    src_y = [(2 * ky + my) * 4 for ky in range(4)]
    src_z = [2 * kz + zh for kz in range(4)]
    src_z = [(div(v, 4) * 8, rem(v, 4)) for v in src_z]
    dest_inner = pz * 8 + (py * 2 + px) * 2 + c
    dest_y = [rem(y + dy, NY) * 4 for dy in range(NY)]
    dest_z = [rem(zl + dz, 4) for dz in range(4)]
    dests = [dest_y[dy] + dest_z[dz] for dy in range(NY) for dz in range(4)]
    cube = div(x, 2) * 16 + div(y, 2) * 4 + div(z, 2)
    stays = dest_inner == inner

    barrier = pltpu.get_barrier_semaphore()
    for d in range(1, GROUP):
        for s in pieces:
            pl.semaphore_signal(barrier, inc=1, device_id=peer(s, d), device_id_type=MESH)
        pl.semaphore_signal(barrier, inc=1, device_id=(inner_at[d], outer), device_id_type=MESH)
    for kx in range(2):
        for ky in range(4):
            for kz in range(4):
                src = (src_z[kz][0] + src_x[kx], src_y[ky] + src_z[kz][1])

                @pl.when((src[0] != inner) | (src[1] != outer))
                def _():
                    pl.semaphore_signal(barrier, inc=1, device_id=src, device_id_type=MESH)

    pl.semaphore_wait(barrier, (GROUP - 1) * (PIECES + 1) + CUBES - stays.astype(jnp.int32))

    def remote(src, dst, send, recv, dev):
        return pltpu.make_async_remote_copy(
            src_ref=src, dst_ref=dst, send_sem=send, recv_sem=recv, device_id=dev, device_id_type=MESH)

    def arrived(ref, sem):
        pltpu.make_async_copy(ref, ref, sem).wait()

    def columns(at, width):
        return pl.ds(pl.multiple_of(at, width), width)

    row_slot = pl.ds(pl.multiple_of(inner * 16, 16), 16)

    for a in range(2):
        pltpu.make_async_copy(
            (enc, dec)[a].at[:, columns(block(0) * BLOCK, BLOCK)], rows.at[a, row_slot, :], row_r).start()
    for e in range(1, 16):
        for a in range(2):
            remote((enc, dec)[a].at[:, columns(inner_block(e) * BLOCK, BLOCK)], rows.at[a, row_slot, :],
                   row_s, row_r, (inner_at[e], outer)).start()
    for d in PEERS:
        for s in pieces:
            for a in range(2):
                remote((acts, cot)[a].at[:, columns(block(d) * BLOCK + s * W, W)], tok.at[a, s, d],
                       tok_s, tok_r.at[a, s, d], peer(s, d)).start()
        for s in pieces:
            remote(ids, idsb.at[s, d], ids_s, ids_r, peer(s, d)).start()
    for s in pieces:
        for a in range(2):
            pltpu.make_async_copy((acts, cot)[a].at[:, columns(block(0) * BLOCK + s * W, W)],
                                  tok.at[a, s, 0], tok_r.at[a, s, 0]).start()
        idsb[s, 0] = ids[...]

    latent = lax.broadcasted_iota(jnp.int32, (LB, 2 * TOK), 0)

    def both(ref, s, d):
        return jnp.concatenate([ref[s, d], ref[s, d + 1]], axis=1)

    def partial(s, d):
        which = both(idsb, s, d)
        hits = [which[k:k + 1, :] == latent for k in range(K)]
        out = []
        for a in range(2):
            full = lax.dot_general(rows[a, :, s * W:(s + 1) * W], tok[a, s, d:d + 2].reshape(2 * TOK, W),
                                   (((1,), (1,)), ((), ())), preferred_element_type=jnp.float32)
            for k in range(K):
                out.append(jnp.sum(jnp.where(hits[k], full, 0.0), axis=0, keepdims=True))
        out = jnp.concatenate(out, axis=0)
        return out[:, :TOK], out[:, TOK:]

    others = pl.ds(1, GROUP - 1)
    arrived(rows, row_r)
    arrived(idsb.at[:, others], ids_r)
    order = []
    for d in PEERS:
        if d & ~1 not in order and d & ~1:
            order.append(d & ~1)
    for d in order + [0]:
        for s in pieces:
            for one in (d, d + 1):
                for a in range(2):
                    arrived(tok.at[a, s, one], tok_r.at[a, s, one])
            for one, value in zip((d, d + 1), partial(s, d)):
                if one == 0:
                    pin[s, 0] = value
                else:
                    pout[s, one] = value
                    remote(pout.at[s, one], pin.at[s, one], p_s, p_r, peer(s, one)).start()

    arrived(rows.at[:, pl.ds(0, LB - 16), :], row_s)
    arrived(idsb.at[:, others], ids_s)
    arrived(tok.at[:, :, others], tok_s)

    arrived(pin.at[:, others], p_r)
    codes = jnp.sum(pin[...].reshape(PIECES * GROUP, 2 * K, TOK), axis=0)
    cout[...] = codes.astype(jnp.bfloat16).astype(jnp.float32)
    for d in PEERS:
        for s in pieces:
            remote(cout, cin.at[s, d], c_s, c_r, peer(s, d)).start()
    for s in pieces:
        cin[s, 0] = cout[...]
    arrived(pout.at[:, others], p_s)
    arrived(cin.at[:, others], c_r)

    for s in pieces:
        for d in range(0, GROUP, 2):
            which, values = both(idsb, s, d), both(cin, s, d)
            hits = [which[k:k + 1, :] == latent for k in range(K)]
            for a in range(2):
                full = jnp.zeros((LB, 2 * TOK), jnp.float32)
                for k in range(K):
                    full = jnp.where(hits[k], values[a * K + k:a * K + k + 1, :], full)
                spread[a, s, :, d * TOK:(d + 2) * TOK] = full.astype(jnp.bfloat16)
        terms = []
        for a in range(2):
            terms.append(lax.dot_general(spread[1 - a, s], tok[a, s].reshape(GROUP * TOK, W),
                                         (((1,), (0,)), ((), ())),
                                         preferred_element_type=jnp.float32).reshape(CUBES, 8, W))
        tsend[:, :, s * W:(s + 1) * W] = jnp.concatenate(terms, axis=1).astype(jnp.bfloat16)

    @pl.when(stays)
    def _():
        pltpu.make_async_copy(tsend.at[outer], fin.at[cube], f_r).start()

    @pl.when(jnp.logical_not(stays))
    def _():
        remote(tsend.at[outer], fin.at[cube], f_s, f_r, (dest_inner, outer)).start()

    for at in dests[1:]:
        remote(tsend.at[at], fin.at[cube], f_s, f_r, (dest_inner, at)).start()
    arrived(cin.at[:, others], c_s)
    arrived(fin, f_r)
    total = jnp.zeros((16, BLOCK), jnp.float32)
    for k in range(CUBES):
        total = total + fin[k].astype(jnp.float32)
    oenc[...] = total[:8]
    odec[...] = total[8:]

    @pl.when(stays)
    def _():
        arrived(tsend.at[pl.ds(1, CUBES - 1)], f_s)

    @pl.when(jnp.logical_not(stays))
    def _():
        arrived(tsend, f_s)


def local(acts, cotangent, latent_ids, enc_rows, dec_rows):
    S, W = PIECES, BLOCK // PIECES
    ids = latent_ids.T
    ids = jnp.concatenate([ids, ids], axis=0)
    vmem, hbm = pl.BlockSpec(memory_space=pltpu.VMEM), pl.BlockSpec(memory_space=pl.ANY)
    dma = pltpu.SemaphoreType.DMA
    return pl.pallas_call(
        kernel,
        out_shape=(jax.ShapeDtypeStruct((8, BLOCK), jnp.float32),) * 2,
        in_specs=[hbm, hbm, vmem, hbm, hbm],
        out_specs=(vmem, vmem),
        scratch_shapes=[
            pltpu.VMEM((2, S, GROUP, TOK, W), jnp.bfloat16),
            pltpu.VMEM((2, LB, BLOCK), jnp.bfloat16),
            pltpu.VMEM((S, GROUP, 8, TOK), jnp.int32),
            pltpu.VMEM((S, GROUP, 8, TOK), jnp.float32),
            pltpu.VMEM((S, GROUP, 8, TOK), jnp.float32),
            pltpu.VMEM((8, TOK), jnp.float32),
            pltpu.VMEM((S, GROUP, 8, TOK), jnp.float32),
            pltpu.VMEM((2, S, LB, GROUP * TOK), jnp.bfloat16),
            pltpu.VMEM((CUBES, 16, BLOCK), jnp.bfloat16),
            pltpu.VMEM((CUBES, 16, BLOCK), jnp.bfloat16),
            dma, dma((2, S, GROUP)),
            dma, dma, dma, dma, dma, dma, dma, dma, dma, dma,
        ],
        compiler_params=pltpu.CompilerParams(
            collective_id=0, has_side_effects=True, vmem_limit_bytes=60 * 2**20),
    )(acts, cotangent, ids, enc_rows, dec_rows)


def solution(mesh):
    placed = (
        P(("inner", "outer"), None),
        P(("inner", "outer"), None),
        P(("inner", "outer"), None),
        P("inner", None),
        P("inner", None),
    )
    return jax.shard_map(
        local,
        mesh=mesh,
        in_specs=placed,
        out_specs=(P("outer", "inner"), P("outer", "inner")),
        check_vma=False,
    )
```

time: 457 us -> 95 us (0.21)
  the two profiles are of different devices: /device:TPU:1 before, /device:TPU:2 now
where the time goes in v2:
time: 95 us; the launch traced here: 94.7 us
  Pallas kernels  90 us (95%)
  local copies, waits for them, and re-layouts  2.65 us (3%)
  other arithmetic  1.36 us (1%)
    pallas_call x1, Pallas kernels, local(): pl.pallas_call(kernel, out_shape=(jax.ShapeDtypeStruct((8, BLOCK), jnp.fl...  90 us
    unnamed x2, local copies, waits for them, and re-layouts  2.65 us

profile of v2, /device:TPU:2, one launch (start us, length us, event | category | flops | bytes accessed | tf_op | source)
XLA Modules:
  0.0 94.7 jit_solution(2139599970536043880)
XLA Ops:
  0.6 1.4 %pad_add_fusion.ids = s32[8,128]{1,0:T(8,128)} fusion(s32[4,128]{1,0:T(4,128)} %bitcast.1), kind=kLoop, calls=%fused_computation | loop fusion | flops 1024 | bytes 6144 | tf_op jit(solution)/shard_map/concatenate | solution.py:228
  2.0 90.0 %shard_map.68 = (f32[8,512]{1,0:T(8,128)}, f32[8,512]{1,0:T(8,128)}) custom-call(bf16[128,8192]{1,0:T(8,128)(2,1)} %acts.1, bf16[128,8192]{1,0:T(8,128)(2,1)} %cot.1, s32[8,128]{1,0:T(8,128)} %pad_add_fusion.ids, bf16[16,8192]{1,0:T(8,128)(2,1)} %enc.1, bf16[16,8192]{1,0:T(8,128)(2,1)} %dec.1), custom_call_target="tpu_custom_call" | custom-call | tf_op jit(solution)/shard_map/pallas_call | solution.py:231
  92.0 1.3 %copy.9 = f32[8,512]{1,0:T(8,128)} copy(f32[8,512]{1,0:T(8,128)} %get-tuple-element.4) | data formatting | bytes 32768
  93.3 1.3 %copy.10 = f32[8,512]{1,0:T(8,128)} copy(f32[8,512]{1,0:T(8,128)} %get-tuple-element.5) | data formatting | bytes 32768

commit v3 on v2

v3 whole, which is shorter than its diff:
```python
import functools

import jax
import jax.numpy as jnp
from jax import lax
from jax.experimental import pallas as pl
from jax.experimental.pallas import tpu as pltpu
from jax.sharding import PartitionSpec as P

MESH = pl.DeviceIdType.MESH
PIECES = 2
NX, NY, NZ = 4, 8, 8
GROUP = 16
CUBES = 32
CHIPS = 8
WINDOW = 8
TOK, LB, BLOCK = 128, 256, 512
K = 4
PEERS = sorted(range(1, GROUP), key=lambda d: (-bin(d >> 1).count("1"), d))


def div(a, b):
    return lax.div(a, jnp.int32(b))


def rem(a, b):
    return lax.rem(a, jnp.int32(b))


def towards(v, s, n):
    return rem(v + (1 - 2 * rem(v, 2)) * (1 - 2 * s) + n, n)


def kernel(acts, cot, ids, enc, dec, oenc, odec,
           tok, rows, idsb, pout, pin, cout, cin, spread, tsend, fin,
           tok_s, tok_r, row_s, row_r, cross_s, cross_r, relay_s, ids_s, ids_r, p_s, p_r, c_s, c_r, f_s, f_r):
    W = BLOCK // PIECES
    inner, outer = lax.axis_index("inner"), lax.axis_index("outer")
    zh, x, c = div(inner, 8), rem(div(inner, 2), 4), rem(inner, 2)
    y, zl = div(outer, 4), rem(outer, 4)
    z = zh * 4 + zl
    me = (inner, outer)
    px, py, pz = rem(x, 2), rem(y, 2), rem(z, 2)
    pieces = range(PIECES)

    cs = (c, 1 - c)
    x2 = [(x * 2, towards(x, s, NX) * 2) for s in pieces]
    y4 = [(y * 4, towards(y, s, NY) * 4) for s in pieces]
    zz = [(z, towards(z, s, NZ)) for s in pieces]
    z8 = [tuple(div(v, 4) * 8 for v in pair) for pair in zz]
    zr = [tuple(rem(v, 4) for v in pair) for pair in zz]
    xc = [[[x2[s][dx] + cs[dc] for dc in range(2)] for dx in range(2)] for s in pieces]
    bx, by, bz = (px * 2, 2 - px * 2), (py * 4, 4 - py * 4), (pz * 8, 8 - pz * 8)
    bxc = [[bx[dx] + cs[dc] for dc in range(2)] for dx in range(2)]
    byz = [[by[dy] + bz[dz] for dz in range(2)] for dy in range(2)]

    def bits(d):
        return d >> 3, (d >> 2) & 1, (d >> 1) & 1, d & 1

    def peer(s, d):
        dx, dy, dz, dc = bits(d)
        return z8[s][dz] + xc[s][dx][dc], y4[s][dy] + zr[s][dz]

    def block(d):
        dx, dy, dz, dc = bits(d)
        return bxc[dx][dc] + byz[dy][dz]

    half = zh * 8
    beside = [half + rem(rem(inner, 8) + e, 8) for e in range(8)]
    across = [8 - half + i for i in range(8)]
    border = (zl == 0) | (zl == 3)
    facing = y * 4 + 3 - zl
    further = y * 4 + rem(zl + 2, 4)

    mx, my = px, div(x, 2)
    src_x = [(2 * kx + mx) * 2 + c for kx in range(2)]
    src_y = [(2 * ky + my) * 4 for ky in range(4)]
    src_z = [2 * kz + zh for kz in range(4)]
    src_z = [(div(v, 4) * 8, rem(v, 4)) for v in src_z]
    dest_inner = pz * 8 + (py * 2 + px) * 2 + c
    dest_y = [rem(y + dy, NY) * 4 for dy in range(NY)]
    dest_z = [rem(zl + dz, 4) for dz in range(4)]
    dests = [dest_y[dy] + dest_z[dz] for dy in range(NY) for dz in range(4)]
    cube = div(x, 2) * 16 + div(y, 2) * 4 + div(z, 2)
    stays = dest_inner == inner

    barrier = pltpu.get_barrier_semaphore()
    for d in range(1, GROUP):
        for s in pieces:
            pl.semaphore_signal(barrier, inc=1, device_id=peer(s, d), device_id_type=MESH)
    for e in range(1, 8):
        pl.semaphore_signal(barrier, inc=1, device_id=(beside[e], outer), device_id_type=MESH)
    pl.semaphore_signal(barrier, inc=1, device_id=(inner, further), device_id_type=MESH)

    @pl.when(border)
    def _():
        for i in across:
            pl.semaphore_signal(barrier, inc=1, device_id=(i, facing), device_id_type=MESH)

    for kx in range(2):
        for ky in range(4):
            for kz in range(4):
                src = (src_z[kz][0] + src_x[kx], src_y[ky] + src_z[kz][1])

                @pl.when((src[0] != inner) | (src[1] != outer))
                def _():
                    pl.semaphore_signal(barrier, inc=1, device_id=src, device_id_type=MESH)

    pl.semaphore_wait(barrier, (GROUP - 1) * PIECES + 8 + CUBES + 8 * border.astype(jnp.int32) - stays.astype(jnp.int32))

    def remote(src, dst, send, recv, dev):
        return pltpu.make_async_remote_copy(
            src_ref=src, dst_ref=dst, send_sem=send, recv_sem=recv, device_id=dev, device_id_type=MESH)

    def arrived(ref, sem):
        pltpu.make_async_copy(ref, ref, sem).wait()

    def columns(at, width):
        return pl.ds(pl.multiple_of(at, width), width)

    row_slot = pl.ds(pl.multiple_of(inner * 16, 16), 16)

    others = pl.ds(1, GROUP - 1)
    near_rows, far_rows = (pl.ds(pl.multiple_of(h, 128), 128) for h in (zh * 128, 128 - zh * 128))

    def chip(t):
        e = rem(t * 3, CHIPS)
        return e, div(e, 4), rem(div(e, 2), 2), rem(e, 2)

    def pick(pair, bit):
        return pair[0] + bit * (pair[1] - pair[0])

    def member(s, t, dc):
        e, dx, dy, dz = chip(t)
        return pick(z8[s], dz) + pick(x2[s], dx) + cs[dc], pick(y4[s], dy) + pick(zr[s], dz)

    def member_block(t, dc):
        e, dx, dy, dz = chip(t)
        return pick(bx, dx) + pick(by, dy) + pick(bz, dz) + cs[dc]

    def send_tokens(t):
        e = chip(t)[0]
        for dc in range(2):
            at = member_block(t, dc) * BLOCK
            for s in pieces:
                for a in range(2):
                    remote((acts, cot)[a].at[:, columns(at + s * W, W)], tok.at[a, s, 2 * e + dc],
                           tok_s.at[a], tok_r.at[a, s, 2 * e + dc], member(s, t, dc)).start()

    def near_tokens(a):
        for s in pieces:
            remote((acts, cot)[a].at[:, columns(block(1) * BLOCK + s * W, W)], tok.at[a, s, 1],
                   tok_s.at[a], tok_r.at[a, s, 1], peer(s, 1)).start()
            pltpu.make_async_copy((acts, cot)[a].at[:, columns(block(0) * BLOCK + s * W, W)],
                                  tok.at[a, s, 0], tok_r.at[a, s, 0]).start()

    for a in (1, 0):
        @pl.when(border)
        def _():
            for n, i in enumerate(across):
                remote((enc, dec)[a].at[:, columns((n % 4 + by[0] + bz[1]) * BLOCK, BLOCK)], rows.at[a, row_slot, :],
                       cross_s.at[a], cross_r.at[a], (i, facing)).start()

        for e in range(1, 8):
            remote((enc, dec)[a].at[:, columns((rem(beside[e], 4) + byz[0][0]) * BLOCK, BLOCK)],
                   rows.at[a, row_slot, :], row_s.at[a], row_r.at[a], (beside[e], outer)).start()
        pltpu.make_async_copy(
            (enc, dec)[a].at[:, columns(block(0) * BLOCK, BLOCK)], rows.at[a, row_slot, :], row_r.at[a]).start()
    for d in PEERS:
        for s in pieces:
            remote(ids, idsb.at[s, d], ids_s, ids_r, peer(s, d)).start()
    for s in pieces:
        idsb[s, 0] = ids[...]
    for a in range(2):
        near_tokens(a)

    @pl.loop(1, WINDOW)
    def _(t):
        send_tokens(t)

    @pl.when(border)
    def _():
        for a in (1, 0):
            arrived(rows.at[a, far_rows, :], cross_r.at[a])
            remote(rows.at[a, far_rows, :], rows.at[a, far_rows, :], relay_s.at[a], cross_r.at[a],
                   (inner, further)).start()

    latent = lax.broadcasted_iota(jnp.int32, (LB, 2 * TOK), 0)
    def both(ref):
        return jnp.concatenate([ref[0], ref[1]], axis=1)

    def partials(t):
        e = chip(t)[0]
        d = 2 * e
        for s in pieces:
            for dc in range(2):
                for a in range(2):
                    arrived(tok.at[a, s, d + dc], tok_r.at[a, s, d + dc])
        @pl.when(t < CHIPS - WINDOW)
        def _():
            send_tokens(t + WINDOW)

        for s in pieces:
            which = both(idsb[s, pl.ds(d, 2)])
            hits = [which[k:k + 1, :] == latent for k in range(K)]
            out = []
            for a in range(2):
                full = lax.dot_general(rows[a, :, s * W:(s + 1) * W], tok[a, s, pl.ds(d, 2)].reshape(2 * TOK, W),
                                       (((1,), (1,)), ((), ())), preferred_element_type=jnp.float32)
                for k in range(K):
                    out.append(jnp.sum(jnp.where(hits[k], full, 0.0), axis=0, keepdims=True))
            out = jnp.concatenate(out, axis=0)
            pout[s, d] = out[:, :TOK]
            pout[s, d + 1] = out[:, TOK:]

        def send(s, dc):
            remote(pout.at[s, d + dc], pin.at[s, d + dc], p_s, p_r, member(s, t, dc)).start()

        @pl.when(t == 0)
        def _():
            for s in pieces:
                pin[s, 0] = pout[s, 0]

        @pl.when(t > 0)
        def _():
            for s in pieces:
                send(s, 0)
        for s in pieces:
            send(s, 1)

    def send_codes():
        arrived(pin.at[:, others], p_r)
        codes = jnp.sum(pin[...].reshape(PIECES * GROUP, 2 * K, TOK), axis=0)
        cout[...] = codes.astype(jnp.bfloat16).astype(jnp.float32)
        for d in PEERS:
            for s in pieces:
                remote(cout, cin.at[s, d], c_s, c_r, peer(s, d)).start()
        for s in pieces:
            cin[s, 0] = cout[...]

    def spread_codes(s):
        @pl.loop(0, CHIPS)
        def _(e):
            which, values = both(idsb[s, pl.ds(2 * e, 2)]), both(cin[s, pl.ds(2 * e, 2)])
            hits = [which[k:k + 1, :] == latent for k in range(K)]
            at = pl.ds(pl.multiple_of(e * 2 * TOK, 2 * TOK), 2 * TOK)
            for a in range(2):
                full = jnp.zeros((LB, 2 * TOK), jnp.float32)
                for k in range(K):
                    full = jnp.where(hits[k], values[a * K + k:a * K + k + 1, :], full)
                spread[a, s, :, at] = full.astype(jnp.bfloat16)

    def term(s):
        out = [lax.dot_general(spread[1 - a, s], tok[a, s].reshape(GROUP * TOK, W), (((1,), (0,)), ((), ())),
                               preferred_element_type=jnp.float32).reshape(CUBES, 8, W) for a in range(2)]
        tsend[s] = jnp.concatenate(out, axis=1).astype(jnp.bfloat16)

    def send_term(s):
        @pl.when(stays)
        def _():
            pltpu.make_async_copy(tsend.at[s, outer], fin.at[s, cube], f_r.at[s]).start()

        @pl.when(jnp.logical_not(stays))
        def _():
            remote(tsend.at[s, outer], fin.at[s, cube], f_s.at[s], f_r.at[s], (dest_inner, outer)).start()

        for at in dests[1:]:
            remote(tsend.at[s, at], fin.at[s, cube], f_s.at[s], f_r.at[s], (dest_inner, at)).start()

    def total(s):
        arrived(fin.at[s], f_r.at[s])
        both_grads = jnp.sum(fin[s].astype(jnp.float32), axis=0)
        oenc[:, s * W:(s + 1) * W] = both_grads[:8]
        odec[:, s * W:(s + 1) * W] = both_grads[8:]

    for a in (1, 0):
        arrived(rows.at[a, near_rows, :], row_r.at[a])

        @pl.when(jnp.logical_not(border))
        def _():
            arrived(rows.at[a, far_rows, :], cross_r.at[a])
    arrived(idsb.at[:, others], ids_r)

    @pl.loop(0, CHIPS)
    def _(t):
        partials(t)

    for a in range(2):
        arrived(rows.at[a, pl.ds(0, LB // 2 - 16), :], row_s.at[a])

        @pl.when(border)
        def _():
            arrived(rows.at[a, far_rows, :], cross_s.at[a])
            arrived(rows.at[a, far_rows, :], relay_s.at[a])
        arrived(tok.at[a, :, others], tok_s.at[a])
    arrived(idsb.at[:, others], ids_s)

    send_codes()
    arrived(pout.at[:, others], p_s)
    arrived(cin.at[:, others], c_r)
    for s in pieces:
        spread_codes(s)
        term(s)
        send_term(s)
    arrived(cin.at[:, others], c_s)
    for s in pieces:
        total(s)
    for s in pieces:
        @pl.when(stays)
        def _():
            arrived(tsend.at[s, pl.ds(1, CUBES - 1)], f_s.at[s])

        @pl.when(jnp.logical_not(stays))
        def _():
            arrived(tsend.at[s], f_s.at[s])


def local(acts, cotangent, latent_ids, enc_rows, dec_rows):
    S, W = PIECES, BLOCK // PIECES
    ids = latent_ids.T
    ids = jnp.concatenate([ids, ids], axis=0)
    vmem, hbm = pl.BlockSpec(memory_space=pltpu.VMEM), pl.BlockSpec(memory_space=pl.ANY)
    dma = pltpu.SemaphoreType.DMA
    two = dma((2,))
    return pl.pallas_call(
        kernel,
        out_shape=(jax.ShapeDtypeStruct((8, BLOCK), jnp.float32),) * 2,
        in_specs=[hbm, hbm, vmem, hbm, hbm],
        out_specs=(vmem, vmem),
        scratch_shapes=[
            pltpu.VMEM((2, S, GROUP, TOK, W), jnp.bfloat16),
            pltpu.VMEM((2, LB, BLOCK), jnp.bfloat16),
            pltpu.VMEM((S, GROUP, 8, TOK), jnp.int32),
            pltpu.VMEM((S, GROUP, 8, TOK), jnp.float32),
            pltpu.VMEM((S, GROUP, 8, TOK), jnp.float32),
            pltpu.VMEM((8, TOK), jnp.float32),
            pltpu.VMEM((S, GROUP, 8, TOK), jnp.float32),
            pltpu.VMEM((2, S, LB, GROUP * TOK), jnp.bfloat16),
            pltpu.VMEM((S, CUBES, 16, W), jnp.bfloat16),
            pltpu.VMEM((S, CUBES, 16, W), jnp.bfloat16),
            two, dma((2, S, GROUP)),
            two, two, two, two, two,
            dma, dma, dma, dma, dma, dma, dma((S,)), dma((S,)),
        ],
        compiler_params=pltpu.CompilerParams(
            collective_id=0, has_side_effects=True, vmem_limit_bytes=60 * 2**20),
    )(acts, cotangent, ids, enc_rows, dec_rows)


def solution(mesh):
    placed = (
        P(("inner", "outer"), None),
        P(("inner", "outer"), None),
        P(("inner", "outer"), None),
        P("inner", None),
        P("inner", None),
    )
    return jax.shard_map(
        local,
        mesh=mesh,
        in_specs=placed,
        out_specs=(P("outer", "inner"), P("outer", "inner")),
        check_vma=False,
    )
```

time: 95 us -> 89.8 us (0.945)
  the two profiles are of different devices: /device:TPU:2 before, /device:TPU:1 now
where the time goes in v3:
time: 89.8 us; the launch traced here: 89.5 us
  Pallas kernels  84.8 us (94%)
  local copies, waits for them, and re-layouts  2.65 us (3%)
  other arithmetic  1.36 us (2%)
    pallas_call x1, Pallas kernels, local(): pl.pallas_call(kernel, out_shape=(jax.ShapeDtypeStruct((8, BLOCK), jnp.fl...  84.8 us
    unnamed x2, local copies, waits for them, and re-layouts  2.65 us

profile of v3, /device:TPU:1, one launch (start us, length us, event | category | flops | bytes accessed | tf_op | source)
XLA Modules:
  0.0 89.5 jit_solution(11347192311967881258)
XLA Ops:
  0.6 1.4 %pad_add_fusion.ids = s32[8,128]{1,0:T(8,128)} fusion(s32[4,128]{1,0:T(4,128)} %bitcast.1), kind=kLoop, calls=%fused_computation | loop fusion | flops 1024 | bytes 6144 | tf_op jit(solution)/shard_map/concatenate | solution.py:321
  2.0 84.8 %shard_map.68 = (f32[8,512]{1,0:T(8,128)}, f32[8,512]{1,0:T(8,128)}) custom-call(bf16[128,8192]{1,0:T(8,128)(2,1)} %acts.1, bf16[128,8192]{1,0:T(8,128)(2,1)} %cot.1, s32[8,128]{1,0:T(8,128)} %pad_add_fusion.ids, bf16[16,8192]{1,0:T(8,128)(2,1)} %enc.1, bf16[16,8192]{1,0:T(8,128)(2,1)} %dec.1), custom_call_target="tpu_custom_call" | custom-call | tf_op jit(solution)/shard_map/pallas_call | solution.py:325
  86.8 1.3 %copy.9 = f32[8,512]{1,0:T(8,128)} copy(f32[8,512]{1,0:T(8,128)} %get-tuple-element.4) | data formatting | bytes 32768
  88.1 1.3 %copy.10 = f32[8,512]{1,0:T(8,128)} copy(f32[8,512]{1,0:T(8,128)} %get-tuple-element.5) | data formatting | bytes 32768

commit v4 on v0

v4 whole, which is shorter than its diff:
```python
import functools

import jax
import jax.numpy as jnp
from jax import lax
from jax.experimental import pallas as pl
from jax.experimental.pallas import tpu as pltpu
from jax.sharding import PartitionSpec as P

MESH = pl.DeviceIdType.MESH
NX, NY, NZ = 4, 8, 8
TOK, LB, BLOCK = 128, 256, 512
HALF = BLOCK // 2
K = 4
SHIFTS = ((0, 0, 0), (1, 0, 0), (-1, 0, 0), (0, 1, 0), (0, -1, 0), (0, 0, 1), (0, 0, -1), (0, 1, 1), (0, -1, -1))
OPPOSITE = (0, 2, 1, 4, 3, 6, 5, 8, 7)
CHIPS = 9
WHOLE = 7
SOURCES = 32


def div(a, b):
    return lax.div(a, jnp.int32(b))


def rem(a, b):
    return lax.rem(a, jnp.int32(b))


def kernel(acts, cot, ids, enc, dec, oenc, odec,
           tok, tokh, rows, idsb, pout, pin, cout, cin, spread, tsend, fin,
           tok_s, tok_r, half_s, half_r, row_s, row_r, cross_s, cross_r, relay_s,
           ids_s, ids_r, p_s, p_r, c_s, c_r, f_s, f_r):
    inner, outer = lax.axis_index("inner"), lax.axis_index("outer")
    zh, x, c = div(inner, 8), rem(div(inner, 2), 4), rem(inner, 2)
    y, zl = div(outer, 4), rem(outer, 4)
    z = zh * 4 + zl
    number = rem(2 * x + y + 3 * z, 8)
    halves = range(2)

    cs = (c, 1 - c)
    xs = {d: rem(x + NX + d, NX) * 2 for d in (-1, 0, 1)}
    ys = {d: rem(y + NY + d, NY) * 4 for d in (-1, 0, 1)}
    zs = {d: rem(z + NZ + d, NZ) for d in (-1, 0, 1)}
    zs = {d: (div(v, 4) * 8, rem(v, 4)) for d, v in zs.items()}

    def member(j, dc):
        dx, dy, dz = SHIFTS[j]
        return zs[dz][0] + xs[dx] + cs[dc], ys[dy] + zs[dz][1]

    def owner(j, dc):
        return member(OPPOSITE[j], dc)

    shift_number = [(2 * dx + dy + 3 * dz) % 8 for dx, dy, dz in SHIFTS]
    owner_number = [rem(number + (8 - n), 8) * 2 for n in shift_number]

    half = zh * 8
    beside = [rem(inner + e, 8) for e in range(8)]
    border = (zl == 0) | (zl == 3)
    facing = y * 4 + 3 - zl
    facing_number = rem(y + 3 * (7 - z), 8)
    further_x = rem(x + NX + jnp.where(zl < 2, 1, -1), NX)
    further = (half + further_x * 2 + c, y * 4 + rem(zl + 2, 4))

    wanted = zh * 4 + x
    dest_inner = number * 2 + c
    dest_y = [rem(y + dy, NY) * 4 for dy in range(NY)]
    dest_z = [rem(zl + dz, 4) for dz in range(4)]
    dests = [dest_y[dy] + dest_z[dz] for dy in range(NY) for dz in range(4)]
    source = x * 8 + z
    stays = dest_inner == inner

    barrier = pltpu.get_barrier_semaphore()
    for j in range(CHIPS):
        for dc in range(2):
            if j or dc:
                pl.semaphore_signal(barrier, inc=1, device_id=member(j, dc), device_id_type=MESH)
    for e in range(1, 8):
        pl.semaphore_signal(barrier, inc=1, device_id=(half + beside[e], outer), device_id_type=MESH)
    pl.semaphore_signal(barrier, inc=1, device_id=further, device_id_type=MESH)

    @pl.when(border)
    def _():
        for i in range(8):
            pl.semaphore_signal(barrier, inc=1, device_id=(8 - half + i, facing), device_id_type=MESH)

    for z1 in range(NZ):
        for x1 in range(NX):
            y1 = rem(wanted + (64 - 2 * x1 - 3 * z1), 8)
            src = ((z1 // 4) * 8 + x1 * 2 + c, y1 * 4 + z1 % 4)

            @pl.when((src[0] != inner) | (src[1] != outer))
            def _():
                pl.semaphore_signal(barrier, inc=1, device_id=src, device_id_type=MESH)

    pl.semaphore_wait(barrier, 2 * CHIPS - 1 + 8 + SOURCES + 8 * border.astype(jnp.int32) - stays.astype(jnp.int32))

    def remote(src, dst, send, recv, dev):
        return pltpu.make_async_remote_copy(
            src_ref=src, dst_ref=dst, send_sem=send, recv_sem=recv, device_id=dev, device_id_type=MESH)

    def arrived(ref, sem):
        pltpu.make_async_copy(ref, ref, sem).wait()

    def columns(at, width):
        return pl.ds(pl.multiple_of(at, width), width)

    row_slot = pl.ds(pl.multiple_of(inner * 16, 16), 16)
    others = pl.ds(1, 2 * CHIPS - 1)
    near_rows, far_rows = (pl.ds(pl.multiple_of(h, 128), 128) for h in (zh * 128, 128 - zh * 128))

    for a in range(2):
        @pl.when(border)
        def _():
            for i in range(8):
                at = rem(facing_number + 2 * (i // 2), 8) * 2 + i % 2
                remote((enc, dec)[a].at[:, columns(at * BLOCK, BLOCK)], rows.at[a, row_slot, :],
                       cross_s.at[a], cross_r.at[a], (8 - half + i, facing)).start()

        for e in range(1, 8):
            at = rem(2 * div(beside[e], 2) + y + 3 * z, 8) * 2 + rem(beside[e], 2)
            remote((enc, dec)[a].at[:, columns(at * BLOCK, BLOCK)],
                   rows.at[a, row_slot, :], row_s.at[a], row_r.at[a], (half + beside[e], outer)).start()
        pltpu.make_async_copy(
            (enc, dec)[a].at[:, columns(dest_inner * BLOCK, BLOCK)], rows.at[a, row_slot, :], row_r.at[a]).start()
    for j in range(CHIPS):
        for dc in range(2):
            if j or dc:
                remote(ids, idsb.at[2 * j + dc], ids_s, ids_r, owner(j, dc)).start()
    idsb[0] = ids[...]
    for j in (7, 8, 0, 1, 2, 3, 4, 5, 6):
        for dc in range(2):
            at = (owner_number[j] + cs[dc]) * BLOCK
            for a in range(2):
                if j >= WHOLE:
                    h = j - WHOLE
                    remote((acts, cot)[a].at[:, columns(at + h * HALF, HALF)], tokh.at[a, h, dc],
                           half_s.at[a], half_r.at[a, h, dc], owner(j, dc)).start()
                elif j or dc:
                    remote((acts, cot)[a].at[:, columns(at, BLOCK)], tok.at[a, 2 * j + dc],
                           tok_s.at[a], tok_r.at[a, 2 * j + dc], owner(j, dc)).start()
                else:
                    pltpu.make_async_copy((acts, cot)[a].at[:, columns(at, BLOCK)], tok.at[a, 0], tok_r.at[a, 0]).start()

    @pl.when(border)
    def _():
        for a in range(2):
            arrived(rows.at[a, far_rows, :], cross_r.at[a])
            remote(rows.at[a, far_rows, :], rows.at[a, far_rows, :], relay_s.at[a], cross_r.at[a], further).start()

    latent = lax.broadcasted_iota(jnp.int32, (LB, 2 * TOK), 0)

    def both(ref):
        return jnp.concatenate([ref[0], ref[1]], axis=1)

    def partials(j, left, right):
        which = both(idsb[pl.ds(2 * j, 2)])
        hits = [which[k:k + 1, :] == latent for k in range(K)]
        out = []
        for a in range(2):
            full = lax.dot_general(left(a), right(a), (((1,), (1,)), ((), ())), preferred_element_type=jnp.float32)
            for k in range(K):
                out.append(jnp.sum(jnp.where(hits[k], full, 0.0), axis=0, keepdims=True))
        out = jnp.concatenate(out, axis=0)
        pout[2 * j] = out[:, :TOK]
        pout[2 * j + 1] = out[:, TOK:]

    def send_partials(j):
        for dc in range(2):
            if j or dc:
                remote(pout.at[2 * j + dc], pin.at[2 * j + dc], p_s, p_r, member(j, dc)).start()
            else:
                pin[0] = pout[0]

    for a in range(2):
        arrived(rows.at[a, near_rows, :], row_r.at[a])

        @pl.when(jnp.logical_not(border))
        def _():
            arrived(rows.at[a, far_rows, :], cross_r.at[a])
    arrived(idsb.at[others], ids_r)

    @pl.loop(0, WHOLE)
    def _(j):
        for a in range(2):
            for dc in range(2):
                arrived(tok.at[a, 2 * j + dc], tok_r.at[a, 2 * j + dc])
        partials(j, lambda a: rows[a], lambda a: tok[a, pl.ds(2 * j, 2)].reshape(2 * TOK, BLOCK))
        for at in range(WHOLE):
            @pl.when(j == at)
            def _():
                send_partials(at)

    for h in halves:
        for a in range(2):
            for dc in range(2):
                arrived(tokh.at[a, h, dc], half_r.at[a, h, dc])
        partials(WHOLE + h, lambda a: rows[a, :, h * HALF:(h + 1) * HALF], lambda a: tokh[a, h].reshape(2 * TOK, HALF))
        send_partials(WHOLE + h)

    for a in range(2):
        arrived(rows.at[a, pl.ds(0, LB // 2 - 16), :], row_s.at[a])

        @pl.when(border)
        def _():
            arrived(rows.at[a, far_rows, :], cross_s.at[a])
            arrived(rows.at[a, far_rows, :], relay_s.at[a])
        arrived(tok.at[a, pl.ds(1, 2 * WHOLE - 1)], tok_s.at[a])
        arrived(tokh.at[a], half_s.at[a])
    arrived(idsb.at[others], ids_s)

    arrived(pin.at[others], p_r)
    codes = jnp.sum(pin[...], axis=0)
    cout[...] = codes.astype(jnp.bfloat16).astype(jnp.float32)
    for j in range(CHIPS):
        for dc in range(2):
            if j or dc:
                remote(cout, cin.at[2 * j + dc], c_s, c_r, owner(j, dc)).start()
    cin[0] = cout[...]
    arrived(pout.at[others], p_s)
    arrived(cin.at[others], c_r)

    @pl.loop(0, CHIPS)
    def _(j):
        which, values = both(idsb[pl.ds(2 * j, 2)]), both(cin[pl.ds(2 * j, 2)])
        hits = [which[k:k + 1, :] == latent for k in range(K)]
        at = columns(j * 2 * TOK, 2 * TOK)
        for a in range(2):
            full = jnp.zeros((LB, 2 * TOK), jnp.float32)
            for k in range(K):
                full = jnp.where(hits[k], values[a * K + k:a * K + k + 1, :], full)
            spread[a, :, at] = full.astype(jnp.bfloat16)

    split = 2 * WHOLE * TOK

    def term(a, h):
        def product(left, right):
            return lax.dot_general(left, right, (((1,), (0,)), ((), ())), preferred_element_type=jnp.float32)

        at = split + h * 2 * TOK
        out = product(spread[1 - a, :, :split], tok[a, :, :, h * HALF:(h + 1) * HALF].reshape(split, HALF))
        out = out + product(spread[1 - a, :, at:at + 2 * TOK], tokh[a, h].reshape(2 * TOK, HALF))
        return out.reshape(SOURCES, 8, HALF)

    for h in halves:
        tsend[h] = jnp.concatenate([term(a, h) for a in range(2)], axis=1).astype(jnp.bfloat16)

        @pl.when(stays)
        def _():
            pltpu.make_async_copy(tsend.at[h, outer], fin.at[h, source], f_r.at[h]).start()

        @pl.when(jnp.logical_not(stays))
        def _():
            remote(tsend.at[h, outer], fin.at[h, source], f_s.at[h], f_r.at[h], (dest_inner, outer)).start()

        for at in dests[1:]:
            remote(tsend.at[h, at], fin.at[h, source], f_s.at[h], f_r.at[h], (dest_inner, at)).start()

    arrived(cin.at[others], c_s)
    for h in halves:
        arrived(fin.at[h], f_r.at[h])
        both_grads = jnp.sum(fin[h].astype(jnp.float32), axis=0)
        oenc[:, h * HALF:(h + 1) * HALF] = both_grads[:8]
        odec[:, h * HALF:(h + 1) * HALF] = both_grads[8:]
    for h in halves:
        @pl.when(stays)
        def _():
            arrived(tsend.at[h, pl.ds(1, SOURCES - 1)], f_s.at[h])

        @pl.when(jnp.logical_not(stays))
        def _():
            arrived(tsend.at[h], f_s.at[h])


def local(acts, cotangent, latent_ids, enc_rows, dec_rows):
    ids = latent_ids.T
    ids = jnp.concatenate([ids, ids], axis=0)
    vmem, hbm = pl.BlockSpec(memory_space=pltpu.VMEM), pl.BlockSpec(memory_space=pl.ANY)
    dma = pltpu.SemaphoreType.DMA
    two = dma((2,))
    return pl.pallas_call(
        kernel,
        out_shape=(jax.ShapeDtypeStruct((8, BLOCK), jnp.float32),) * 2,
        in_specs=[hbm, hbm, vmem, hbm, hbm],
        out_specs=(vmem, vmem),
        scratch_shapes=[
            pltpu.VMEM((2, 2 * WHOLE, TOK, BLOCK), jnp.bfloat16),
            pltpu.VMEM((2, 2, 2, TOK, HALF), jnp.bfloat16),
            pltpu.VMEM((2, LB, BLOCK), jnp.bfloat16),
            pltpu.VMEM((2 * CHIPS, 8, TOK), jnp.int32),
            pltpu.VMEM((2 * CHIPS, 8, TOK), jnp.float32),
            pltpu.VMEM((2 * CHIPS, 8, TOK), jnp.float32),
            pltpu.VMEM((8, TOK), jnp.float32),
            pltpu.VMEM((2 * CHIPS, 8, TOK), jnp.float32),
            pltpu.VMEM((2, LB, 2 * CHIPS * TOK), jnp.bfloat16),
            pltpu.VMEM((2, SOURCES, 16, HALF), jnp.bfloat16),
            pltpu.VMEM((2, SOURCES, 16, HALF), jnp.bfloat16),
            two, dma((2, 2 * WHOLE)), two, dma((2, 2, 2)),
            two, two, two, two, two,
            dma, dma, dma, dma, dma, dma, two, two,
        ],
        compiler_params=pltpu.CompilerParams(
            collective_id=0, has_side_effects=True, vmem_limit_bytes=60 * 2**20),
    )(acts, cotangent, ids, enc_rows, dec_rows)


def solution(mesh):
    placed = (
        P(("inner", "outer"), None),
        P(("inner", "outer"), None),
        P(("inner", "outer"), None),
        P("inner", None),
        P("inner", None),
    )
    return jax.shard_map(
        local,
        mesh=mesh,
        in_specs=placed,
        out_specs=(P("outer", "inner"), P("outer", "inner")),
        check_vma=False,
    )
```

time: 457 us -> 80.1 us (0.18)
  blocking collectives: 217 us -> 0 us
  waiting for transfers between devices: 165 us -> 0 us
  Pallas kernels: 0 us -> 75.1 us
  local copies, waits for them, and re-layouts: 22.8 us -> 2.65 us
  matrix products: 19.1 us -> 0 us
  other arithmetic: 17.4 us -> 1.36 us
  between operations: 14.1 us -> 0.64 us
    all_to_all x2 -> x0, blocking collectives: 217 us -> none  [the longest x1 193 us: local(): lax.all_to_all(values, 'inner', split_axis=3, concat_axis=0, tiled=True)]
    all_gather x2 -> x0, waiting for transfers between devices: 164 us -> none  [the longest x1 91 us: local(): lax.all_gather(enc_rows, 'inner', axis=0, tiled=True)]
    pallas_call x0 -> x1, Pallas kernels: none -> 75.1 us  [local(): pl.pallas_call(kernel, out_shape=(jax.ShapeDtypeStruct((8, BLOCK), jnp.fl...]
    another operation x1 -> x0, local copies, waits for them, and re-layouts: 21 us -> none  [local(): values = jnp.stack([term_enc, term_dec])[None].astype(jnp.bfloat16)]
    dot_general x2 -> x0, matrix products: 19.1 us -> none  [the longest x1 9.58 us: local(): lax.dot_general(dcodes, acts, over_tokens, preferred_element_type=jnp.flo...]
    reduce_sum x2 -> x0, other arithmetic: 9.13 us -> none  [the longest x1 8.69 us: local(): section_sum = jnp.sum(received.astype(jnp.float32), axis=0)]
    another operation x1 -> x0, other arithmetic: 7.45 us -> none  [local(): values = jnp.stack([term_enc, term_dec])[None].astype(jnp.bfloat16)]
  transfers between devices with their start and end apart: 2 -> 0, of which waited for: 2 -> 0; matrix products, arithmetic and copies ran while one was open for 2% -> 0% of each run, Pallas kernels for 0% -> 0%
where the time goes in v4:
time: 80.1 us; the launch traced here: 79.7 us
  Pallas kernels  75.1 us (94%)
  local copies, waits for them, and re-layouts  2.65 us (3%)
  other arithmetic  1.36 us (2%)
    pallas_call x1, Pallas kernels, local(): pl.pallas_call(kernel, out_shape=(jax.ShapeDtypeStruct((8, BLOCK), jnp.fl...  75.1 us
    unnamed x2, local copies, waits for them, and re-layouts  2.65 us

profile of v4, /device:TPU:1, one launch (start us, length us, event | category | flops | bytes accessed | tf_op | source)
XLA Modules:
  0.0 79.7 jit_solution(2289784876457473862)
XLA Ops:
  0.6 1.4 %pad_add_fusion.ids = s32[8,128]{1,0:T(8,128)} fusion(s32[4,128]{1,0:T(4,128)} %bitcast.1), kind=kLoop, calls=%fused_computation | loop fusion | flops 1024 | bytes 6144 | tf_op jit(solution)/shard_map/concatenate | solution.py:277
  2.0 75.1 %shard_map.68 = (f32[8,512]{1,0:T(8,128)}, f32[8,512]{1,0:T(8,128)}) custom-call(bf16[128,8192]{1,0:T(8,128)(2,1)} %acts.1, bf16[128,8192]{1,0:T(8,128)(2,1)} %cot.1, s32[8,128]{1,0:T(8,128)} %pad_add_fusion.ids, bf16[16,8192]{1,0:T(8,128)(2,1)} %enc.1, bf16[16,8192]{1,0:T(8,128)(2,1)} %dec.1), custom_call_target="tpu_custom_call" | custom-call | tf_op jit(solution)/shard_map/pallas_call | solution.py:281
  77.1 1.3 %copy.9 = f32[8,512]{1,0:T(8,128)} copy(f32[8,512]{1,0:T(8,128)} %get-tuple-element.4) | data formatting | bytes 32768
  78.4 1.3 %copy.10 = f32[8,512]{1,0:T(8,128)} copy(f32[8,512]{1,0:T(8,128)} %get-tuple-element.5) | data formatting | bytes 32768

commit v5 on v4

--- a/solution.py
+++ b/solution.py
@@ -70,6 +70,18 @@
     source = x * 8 + z
     stays = dest_inner == inner
 
+    def columns(at, width):
+        return pl.ds(pl.multiple_of(at, width), width)
+
+    row_slot = pl.ds(pl.multiple_of(inner * 16, 16), 16)
+
+    for a in range(2):
+        pltpu.make_async_copy(
+            (enc, dec)[a].at[:, columns(dest_inner * BLOCK, BLOCK)], rows.at[a, row_slot, :], row_r.at[a]).start()
+        pltpu.make_async_copy(
+            (acts, cot)[a].at[:, columns(dest_inner * BLOCK, BLOCK)], tok.at[a, 0], tok_r.at[a, 0]).start()
+    idsb[0] = ids[...]
+
     barrier = pltpu.get_barrier_semaphore()
     for j in range(CHIPS):
         for dc in range(2):
@@ -102,10 +114,6 @@
     def arrived(ref, sem):
         pltpu.make_async_copy(ref, ref, sem).wait()
 
-    def columns(at, width):
-        return pl.ds(pl.multiple_of(at, width), width)
-
-    row_slot = pl.ds(pl.multiple_of(inner * 16, 16), 16)
     others = pl.ds(1, 2 * CHIPS - 1)
     near_rows, far_rows = (pl.ds(pl.multiple_of(h, 128), 128) for h in (zh * 128, 128 - zh * 128))
 
@@ -121,13 +129,10 @@
             at = rem(2 * div(beside[e], 2) + y + 3 * z, 8) * 2 + rem(beside[e], 2)
             remote((enc, dec)[a].at[:, columns(at * BLOCK, BLOCK)],
                    rows.at[a, row_slot, :], row_s.at[a], row_r.at[a], (half + beside[e], outer)).start()
-        pltpu.make_async_copy(
-            (enc, dec)[a].at[:, columns(dest_inner * BLOCK, BLOCK)], rows.at[a, row_slot, :], row_r.at[a]).start()
     for j in range(CHIPS):
         for dc in range(2):
             if j or dc:
                 remote(ids, idsb.at[2 * j + dc], ids_s, ids_r, owner(j, dc)).start()
-    idsb[0] = ids[...]
     for j in (7, 8, 0, 1, 2, 3, 4, 5, 6):
         for dc in range(2):
             at = (owner_number[j] + cs[dc]) * BLOCK
@@ -139,8 +144,6 @@
                 elif j or dc:
                     remote((acts, cot)[a].at[:, columns(at, BLOCK)], tok.at[a, 2 * j + dc],
                            tok_s.at[a], tok_r.at[a, 2 * j + dc], owner(j, dc)).start()
-                else:
-                    pltpu.make_async_copy((acts, cot)[a].at[:, columns(at, BLOCK)], tok.at[a, 0], tok_r.at[a, 0]).start()
 
     @pl.when(border)
     def _():
@@ -180,23 +183,26 @@
             arrived(rows.at[a, far_rows, :], cross_r.at[a])
     arrived(idsb.at[others], ids_r)
 
-    @pl.loop(0, WHOLE)
-    def _(j):
-        for a in range(2):
-            for dc in range(2):
-                arrived(tok.at[a, 2 * j + dc], tok_r.at[a, 2 * j + dc])
-        partials(j, lambda a: rows[a], lambda a: tok[a, pl.ds(2 * j, 2)].reshape(2 * TOK, BLOCK))
-        for at in range(WHOLE):
-            @pl.when(j == at)
-            def _():
-                send_partials(at)
-
-    for h in halves:
-        for a in range(2):
-            for dc in range(2):
-                arrived(tokh.at[a, h, dc], half_r.at[a, h, dc])
-        partials(WHOLE + h, lambda a: rows[a, :, h * HALF:(h + 1) * HALF], lambda a: tokh[a, h].reshape(2 * TOK, HALF))
-        send_partials(WHOLE + h)
+    def left(j):
+        h = j - WHOLE
+        return lambda a: rows[a] if j < WHOLE else rows[a, :, h * HALF:(h + 1) * HALF]
+
+    def right(j):
+        return lambda a: (tok[a, 2 * j:2 * j + 2].reshape(2 * TOK, BLOCK) if j < WHOLE else
+                          tokh[a, j - WHOLE].reshape(2 * TOK, HALF))
+
+    for group in ((0, 1, 2), (3, 4, 5), (6, 7, 8)):
+        for j in group:
+            for a in range(2):
+                for dc in range(2):
+                    if j < WHOLE:
+                        arrived(tok.at[a, 2 * j + dc], tok_r.at[a, 2 * j + dc])
+                    else:
+                        arrived(tokh.at[a, j - WHOLE, dc], half_r.at[a, j - WHOLE, dc])
+        for j in group:
+            partials(j, left(j), right(j))
+        for j in group:
+            send_partials(j)
 
     for a in range(2):
         arrived(rows.at[a, pl.ds(0, LB // 2 - 16), :], row_s.at[a])
@@ -220,16 +226,19 @@
     arrived(pout.at[others], p_s)
     arrived(cin.at[others], c_r)
 
+    latent16 = latent.astype(jnp.float32).astype(jnp.bfloat16)
+
     @pl.loop(0, CHIPS)
     def _(j):
-        which, values = both(idsb[pl.ds(2 * j, 2)]), both(cin[pl.ds(2 * j, 2)])
-        hits = [which[k:k + 1, :] == latent for k in range(K)]
+        which = both(idsb[pl.ds(2 * j, 2)]).astype(jnp.float32).astype(jnp.bfloat16)
+        values = both(cin[pl.ds(2 * j, 2)]).astype(jnp.bfloat16)
+        hits = [which[k:k + 1, :] == latent16 for k in range(K)]
         at = columns(j * 2 * TOK, 2 * TOK)
         for a in range(2):
-            full = jnp.zeros((LB, 2 * TOK), jnp.float32)
+            full = jnp.zeros((LB, 2 * TOK), jnp.bfloat16)
             for k in range(K):
                 full = jnp.where(hits[k], values[a * K + k:a * K + k + 1, :], full)
-            spread[a, :, at] = full.astype(jnp.bfloat16)
+            spread[a, :, at] = full
 
     split = 2 * WHOLE * TOK
 
@@ -274,7 +283,6 @@
 
 def local(acts, cotangent, latent_ids, enc_rows, dec_rows):
     ids = latent_ids.T
-    ids = jnp.concatenate([ids, ids], axis=0)
     vmem, hbm = pl.BlockSpec(memory_space=pltpu.VMEM), pl.BlockSpec(memory_space=pl.ANY)
     dma = pltpu.SemaphoreType.DMA
     two = dma((2,))
@@ -287,7 +295,7 @@
             pltpu.VMEM((2, 2 * WHOLE, TOK, BLOCK), jnp.bfloat16),
             pltpu.VMEM((2, 2, 2, TOK, HALF), jnp.bfloat16),
             pltpu.VMEM((2, LB, BLOCK), jnp.bfloat16),
-            pltpu.VMEM((2 * CHIPS, 8, TOK), jnp.int32),
+            pltpu.VMEM((2 * CHIPS, K, TOK), jnp.int32),
             pltpu.VMEM((2 * CHIPS, 8, TOK), jnp.float32),
             pltpu.VMEM((2 * CHIPS, 8, TOK), jnp.float32),
             pltpu.VMEM((8, TOK), jnp.float32),

time: 80.1 us -> 75.6 us (0.944)
  Pallas kernels: 75.1 us -> 72 us
  other arithmetic: 1.36 us -> 0 us
    pallas_call x1, Pallas kernels: 75.1 us -> 72 us  [local(): pl.pallas_call(kernel, out_shape=(jax.ShapeDtypeStruct((8, BLOCK), jnp.fl...]
    concatenate x1 -> x0, other arithmetic: 1.36 us -> none  [local(): ids = jnp.concatenate([ids, ids], axis=0)]
where the time goes in v5:
time: 75.6 us; the launch traced here: 75.3 us
  Pallas kernels  72 us (95%)
  local copies, waits for them, and re-layouts  2.65 us (4%)
    pallas_call x1, Pallas kernels, local(): pl.pallas_call(kernel, out_shape=(jax.ShapeDtypeStruct((8, BLOCK), jnp.fl...  72 us
    unnamed x2, local copies, waits for them, and re-layouts  2.65 us

profile of v5, /device:TPU:1, one launch (start us, length us, event | category | flops | bytes accessed | tf_op | source)
XLA Modules:
  0.0 75.3 jit_solution(13748388983197363501)
XLA Ops:
  0.6 72.0 %shard_map.68 = (f32[8,512]{1,0:T(8,128)}, f32[8,512]{1,0:T(8,128)}) custom-call(bf16[128,8192]{1,0:T(8,128)(2,1)} %acts.1, bf16[128,8192]{1,0:T(8,128)(2,1)} %cot.1, s32[4,128]{1,0:T(4,128)} %bitcast.1, bf16[16,8192]{1,0:T(8,128)(2,1)} %enc.1, bf16[16,8192]{1,0:T(8,128)(2,1)} %dec.1), custom_call_target="tpu_custom_call" | custom-call | tf_op jit(solution)/shard_map/pallas_call | solution.py:289
  72.7 1.3 %copy.9 = f32[8,512]{1,0:T(8,128)} copy(f32[8,512]{1,0:T(8,128)} %get-tuple-element.4) | data formatting | bytes 32768
  74.0 1.3 %copy.10 = f32[8,512]{1,0:T(8,128)} copy(f32[8,512]{1,0:T(8,128)} %get-tuple-element.5) | data formatting | bytes 32768

commit v6 on v5

--- a/solution.py
+++ b/solution.py
@@ -228,12 +228,11 @@
 
     latent16 = latent.astype(jnp.float32).astype(jnp.bfloat16)
 
-    @pl.loop(0, CHIPS)
-    def _(j):
+    for j in range(CHIPS):
         which = both(idsb[pl.ds(2 * j, 2)]).astype(jnp.float32).astype(jnp.bfloat16)
         values = both(cin[pl.ds(2 * j, 2)]).astype(jnp.bfloat16)
         hits = [which[k:k + 1, :] == latent16 for k in range(K)]
-        at = columns(j * 2 * TOK, 2 * TOK)
+        at = pl.ds(2 * TOK * j, 2 * TOK)
         for a in range(2):
             full = jnp.zeros((LB, 2 * TOK), jnp.bfloat16)
             for k in range(K):

time: 75.6 us -> 74.9 us (level)
  no operation moved by 1% of the time
where the time goes in v6:
time: 74.9 us; the launch traced here: 74.6 us
  Pallas kernels  71.3 us (95%)
  local copies, waits for them, and re-layouts  2.65 us (4%)
    pallas_call x1, Pallas kernels, local(): pl.pallas_call(kernel, out_shape=(jax.ShapeDtypeStruct((8, BLOCK), jnp.fl...  71.3 us
    unnamed x2, local copies, waits for them, and re-layouts  2.65 us

profile of v6, /device:TPU:1, one launch (start us, length us, event | category | flops | bytes accessed | tf_op | source)
XLA Modules:
  0.0 74.6 jit_solution(9343734196659613572)
XLA Ops:
  0.6 71.3 %shard_map.68 = (f32[8,512]{1,0:T(8,128)}, f32[8,512]{1,0:T(8,128)}) custom-call(bf16[128,8192]{1,0:T(8,128)(2,1)} %acts.1, bf16[128,8192]{1,0:T(8,128)(2,1)} %cot.1, s32[4,128]{1,0:T(4,128)} %bitcast.1, bf16[16,8192]{1,0:T(8,128)(2,1)} %enc.1, bf16[16,8192]{1,0:T(8,128)(2,1)} %dec.1), custom_call_target="tpu_custom_call" | custom-call | tf_op jit(solution)/shard_map/pallas_call | solution.py:288
  72.0 1.3 %copy.9 = f32[8,512]{1,0:T(8,128)} copy(f32[8,512]{1,0:T(8,128)} %get-tuple-element.4) | data formatting | bytes 32768
  73.3 1.3 %copy.10 = f32[8,512]{1,0:T(8,128)} copy(f32[8,512]{1,0:T(8,128)} %get-tuple-element.5) | data formatting | bytes 32768
